TPU v7x, 512 devices: a whole 4x4x16 slice. The times are simulated.
512 devices in a mesh: row: 64 (over x, z), col: 8 (over y, core).
Axes of the slice: x: 4, y: 4, z: 16, core: 2. Of those that a mesh axis runs over, the one named last changes fastest.
Arguments:
- coarse_kernel: bfloat16 [32768, 2048], P('row', 'col'), may hold values from -6 to 6
- row_cond: bfloat16 [1024, 8, 16], P(('row', 'col')), may hold values from -1.796875 to 1.796875
- row_val: bfloat16 [1024, 4, 8], P(('row', 'col')), may hold values from -1.796875 to 1.796875
- col_cond: bfloat16 [64, 8, 16], P('col'), may hold values from -1.796875 to 1.796875
- col_val: bfloat16 [64, 4, 8], P('col'), may hold values from -1.796875 to 1.796875
- near_row: int32 [1024], replicated, may hold values from 0 to 255, as said below
- owner_map: int32 [256], replicated, may hold values from 0 to 255, as said below
- near_col: int32 [64], P('col'), may hold values from 0 to 1
Outputs:
- fine_kernel: bfloat16 [32768, 2048], P('row', 'col')
Inputs may be any that keep to these rules, and one draw needn't show every extreme that they name: Fine row r's coarse point is stored on row index owner_map[near_row[r]] // 4. Among the 16 fine rows of one row index at most 2 have their coarse point on one row index, and in every such block some row index serves exactly 2 of them. `owner_map`: A permutation: every slot holds one coarse row k-point.
All inputs are finite; a program needn't handle non-finite values.
Results may differ from a plain program's by a relative error of at most 0.0057.
Values may be sent and summed in bfloat16 or wider, within the bound.
A program may use at most 128 MiB of HBM per device.

v0:
```python
import jax
import jax.numpy as jnp
from jax import lax
from jax.sharding import PartitionSpec as P


def expand_pairs(conduction, valence):
    entries = conduction.shape[0]
    product = (
        conduction.astype(jnp.float32)[:, :, None, :, None]
        * valence.astype(jnp.float32)[:, None, :, None, :]
    )
    return product.reshape(
        entries, conduction.shape[1] * valence.shape[1], conduction.shape[2] * valence.shape[2]
    ).astype(jnp.bfloat16)


def shards(coarse_kernel, row_cond, row_val, col_cond, col_val, near_row, owner_map, near_col):
    groups = lax.axis_size("row")
    own_index = lax.axis_index("row")
    cond_rows, val_rows = (
        lax.all_gather(row_cond, "col", axis=0, tiled=True),
        lax.all_gather(row_val, "col", axis=0, tiled=True),
    )
    left_pairs = expand_pairs(cond_rows, val_rows)
    right_pairs = expand_pairs(col_cond, col_val)
    fine_rows = left_pairs.shape[0]
    fine_trans = left_pairs.shape[1]
    coarse_trans = left_pairs.shape[2]
    fine_cols = right_pairs.shape[0]
    span = coarse_kernel.shape[1] // coarse_trans
    per_owner = coarse_kernel.shape[0] // coarse_trans
    capacity = 2 * ((fine_rows + groups - 1) // groups)
    width = fine_cols * fine_trans
    placed = (near_col[:, None] == jnp.arange(span, dtype=jnp.int32)[None, :]).astype(jnp.bfloat16)
    spread = jnp.einsum("fc,ftb->cbft", placed, right_pairs, preferred_element_type=jnp.float32)
    spread = spread.reshape(span * coarse_trans, width).astype(jnp.bfloat16)
    storage = jnp.take(owner_map, near_row)
    owner_grid = (storage // per_owner).reshape(groups, fine_rows)
    point_grid = (storage % per_owner).reshape(groups, fine_rows)
    positions = jnp.arange(fine_rows, dtype=jnp.int32)
    earlier = positions[None, :] < positions[:, None]
    matches = (owner_grid[:, :, None] == owner_grid[:, None, :]) & earlier[None, :, :]
    rank_grid = jnp.sum(matches.astype(jnp.int32), axis=2)
    my_owner = lax.dynamic_index_in_dim(owner_grid, own_index, 0, keepdims=False)
    my_rank = lax.dynamic_index_in_dim(rank_grid, own_index, 0, keepdims=False)
    slot_ids = jnp.arange(capacity, dtype=jnp.int32)
    landing = my_owner * capacity + my_rank
    chosen = (owner_grid[:, None, :] == own_index) & (
        rank_grid[:, None, :] == slot_ids[None, :, None]
    )
    wanted = jnp.sum(jnp.where(chosen, point_grid[:, None, :], 0), axis=2)
    stored_blocks = coarse_kernel.reshape(per_owner, coarse_trans, span * coarse_trans)
    outgoing = jnp.take(stored_blocks, wanted, axis=0)
    received = lax.all_to_all(outgoing, "row", split_axis=0, concat_axis=0, tiled=True)
    fetched = jnp.take(
        received.reshape(groups * capacity, coarse_trans, span * coarse_trans), landing, axis=0
    )
    partial_value = jnp.einsum(
        "rta,raw->rtw", left_pairs, fetched, preferred_element_type=jnp.float32
    )
    result = jnp.dot(
        partial_value.reshape(fine_rows * fine_trans, span * coarse_trans),
        spread.astype(jnp.float32),
        precision=lax.Precision.HIGHEST,
        preferred_element_type=jnp.float32,
    )
    return result.astype(jnp.bfloat16)


def solution(mesh):
    return jax.shard_map(
        shards,
        mesh=mesh,
        in_specs=(
            P("row", "col"),
            P(("row", "col"), None, None),
            P(("row", "col"), None, None),
            P("col", None, None),
            P("col", None, None),
            P(),
            P(),
            P("col"),
        ),
        out_specs=P("row", "col"),
        check_vma=False,
    )
```

profile of v0, /device:TPU:1, one launch (start us, length us, event | category | flops | bytes accessed | tf_op | source)
XLA Modules:
  0.0 412.9 jit_solution(12486664833564626080)
XLA Ops:
  0.0 0.0 copy-start
  0.0 0.7 fusion.11
  0.8 6.2 %gather_fusion = s32[1024]{0:T(1024)S(1)} fusion(s32[256]{0:T(256)} %param.14, s32[1024]{0:T(1024)S(1)} %fusion.11), kind=kCustom, calls=%fused_computation | custom fusion | bytes 12288 | tf_op jit(solution)/shard_map/jit(_take)/gather | solution.py:38
  6.9 0.7 and_select_fusion
  7.6 0.1 select_n.107
  7.7 0.1 copy.41
  7.8 0.1 convert_reduce_fusion
  8.0 0.1 copy.46
  8.1 0.1 reshape.209
  8.2 0.1 copy.45
  8.3 0.0 copy-done
  8.3 6.3 %gather_fusion.1 = bf16[128,128,256]{2,1,0:T(8,128)(2,1)} fusion(bf16[4,128,256]{2,1,0:T(8,128)(2,1)S(1)} %bitcast.25, s32[1024]{0:T(1024)S(1)} %pad_clamp_fusion.1), kind=kCustom, calls=%fused_computation.1 | custom fusion | bytes 16777728 | tf_op jit(solution)/shard_map/jit(_take)/gather | solution.py:54
  14.6 7.4 %broadcast_select_fusion = bf16[64,2,128,256]{3,2,1,0:T(8,128)(2,1)} fusion(bf16[64,2,128,256]{3,2,1,0:T(8,128)(2,1)} %bitcast.26, pred[64,2]{1,0:T(8,128)(4,1)S(1)} %copy.45), kind=kLoop, calls=%fused_computation.3 | loop fusion | flops 4194304 | bytes 16777344 | tf_op jit(solution)/shard_map/jit(_take)/select_n | solution.py:54
  22.0 0.0 copy-start.5
  22.0 19.5 %all-to-all-start = ((bf16[64,2,128,256]{3,2,1,0:T(8,128)(2,1)}), bf16[64,2,128,256]{3,2,1,0:T(8,128)(2,1)}, u32[]{:S(2)}, u32[]{:S(2)}) async-start(bf16[64,2,128,256]{3,2,1,0:T(8,128)(2,1)} %broadcast_select_fusion), calls=%async_computation | async-start | bytes 16777216 | tf_op jit(solution)/shard_map/all_to_all | solution.py:55
  41.6 0.0 copy-done.3
  41.6 14.1 %all_gather.6 = bf16[16,8,16]{2,1,0:T(8,128)(2,1)S(1)} all-gather(bf16[2,8,16]{2,1,0:T(8,128)(2,1)S(1)} %copy-done.3), channel_id=1, replica_groups=mesh['row'=64,'col'=8] {'col'}, dimensions={0}, use_global_device_ids=true | all-gather | bytes 4608 | tf_op jit(solution)/shard_map/all_gather | solution.py:22
  55.7 0.1 copy.39
  55.8 0.0 copy-done.4
  55.8 11.2 %all_gather.7 = bf16[16,4,8]{2,1,0:T(4,128)(2,1)S(1)} all-gather(bf16[2,4,8]{2,1,0:T(4,128)(2,1)S(1)} %copy-done.4), channel_id=1, replica_groups=mesh['row'=64,'col'=8] {'col'}, dimensions={0}, use_global_device_ids=true | all-gather | bytes 1152 | tf_op jit(solution)/shard_map/all_gather | solution.py:23
  67.0 0.1 copy.40
  67.1 0.3 multiply_convert_fusion.1
  67.4 0.4 copy.47
  67.9 0.2 fusion
  68.1 1.0 reshape.198
  69.1 0.2 add_reduce_fusion
  69.4 0.1 fusion.10
  69.4 0.2 multiply_convert_fusion.2
  69.6 337.8 %all-to-all-done = bf16[64,2,128,256]{3,2,1,0:T(8,128)(2,1)} async-done(((bf16[64,2,128,256]{3,2,1,0:T(8,128)(2,1)}), bf16[64,2,128,256]{3,2,1,0:T(8,128)(2,1)}, u32[]{:S(2)}, u32[]{:S(2)}) %all-to-all-start) | async-done | bytes 8388640 | tf_op jit(solution)/shard_map/all_to_all | solution.py:55
  407.4 4.0 gather_fusion.2
  411.4 0.3 fusion.1
  411.8 1.1 convolution_convert_fusion
  (20 shorter events, 0.1 us)
Async XLA Ops:
  0.0 8.3 %copy-start = (bf16[512,256]{1,0:T(8,128)(2,1)S(1)}, bf16[512,256]{1,0:T(8,128)(2,1)}, u32[]{:S(2)}) copy-start(bf16[512,256]{1,0:T(8,128)(2,1)} %param.8) | copy-start | bytes 786436
  22.0 19.6 %copy-start.3 = (bf16[2,8,16]{2,1,0:T(8,128)(2,1)S(1)}, bf16[2,8,16]{2,1,0:T(8,128)(2,1)}, u32[]{:S(2)}) copy-start(bf16[2,8,16]{2,1,0:T(8,128)(2,1)} %param.9) | copy-start | bytes 1540
  22.0 33.8 %copy-start.4 = (bf16[2,4,8]{2,1,0:T(4,128)(2,1)S(1)}, bf16[2,4,8]{2,1,0:T(4,128)(2,1)}, u32[]{:S(2)}) copy-start(bf16[2,4,8]{2,1,0:T(4,128)(2,1)} %param.10) | copy-start | bytes 388
  22.0 45.8 %copy-start.1 = (bf16[8,8,16]{2,1,0:T(8,128)(2,1)S(1)}, bf16[8,8,16]{2,1,0:T(8,128)(2,1)}, u32[]{:S(2)}) copy-start(bf16[8,8,16]{2,1,0:T(8,128)(2,1)} %param.11) | copy-start | bytes 6148
  22.0 45.8 %copy-start.2 = (bf16[8,4,8]{2,1,0:T(4,128)(2,1)S(1)}, bf16[8,4,8]{2,1,0:T(4,128)(2,1)}, u32[]{:S(2)}) copy-start(bf16[8,4,8]{2,1,0:T(4,128)(2,1)} %param.12) | copy-start | bytes 1540
  22.0 47.3 %copy-start.5 = (s32[8]{0:T(128)S(1)}, s32[8]{0:T(128)}, u32[]{:S(2)}) copy-start(s32[8]{0:T(128)} %param.15) | copy-start | bytes 100
  22.0 385.4 %all-to-all-start = ((bf16[64,2,128,256]{3,2,1,0:T(8,128)(2,1)}), bf16[64,2,128,256]{3,2,1,0:T(8,128)(2,1)}, u32[]{:S(2)}, u32[]{:S(2)}) async-start(bf16[64,2,128,256]{3,2,1,0:T(8,128)(2,1)} %broadcast_select_fusion), calls=%async_computation | async-start | bytes 16777216 | tf_op jit(solution)/shard_map/all_to_all | solution.py:55
where the time goes:
time: 415 us; the launch traced here: 413 us
  waiting for transfers between devices  338 us (81%)
  blocking collectives  25.3 us (6%)
  starting transfers between devices  19.5 us (5%)
  local copies, waits for them, and re-layouts  18.6 us (4%)
  other arithmetic  9.97 us (2%)
    all_to_all x1, waiting for transfers between devices, shards(): lax.all_to_all(outgoing, 'row', split_axis=0, concat_axis=0, tiled=True)  338 us
    all_to_all x1, starting transfers between devices, shards(): lax.all_to_all(outgoing, 'row', split_axis=0, concat_axis=0, tiled=True)  19.5 us
    all_gather x1, blocking collectives, shards(): lax.all_gather(row_cond, 'col', axis=0, tiled=True)  14.1 us
    all_gather x1, blocking collectives, shards(): lax.all_gather(row_val, 'col', axis=0, tiled=True)  11.2 us
  transfers between devices with their start and end apart: 1, of which 1 were waited for; matrix products, arithmetic and copies ran while one was open for 1% of the time, Pallas kernels for 0%

commit v1 on v0

v1 whole, which is shorter than its diff:
```python
import functools

import jax
import jax.numpy as jnp
from jax import lax
from jax.experimental import pallas as pl
from jax.experimental.pallas import tpu as pltpu
from jax.sharding import PartitionSpec as P

MESH = pl.DeviceIdType.MESH
F32 = jnp.float32
BF16 = jnp.bfloat16
Z_SIZE = 16


def one_hot(shape, test):
    rows = lax.broadcasted_iota(jnp.int32, shape, 0)
    lanes = lax.broadcasted_iota(jnp.int32, shape, 1)
    return jnp.where(test(rows, lanes), 1.0, 0.0).astype(BF16)


def mm(a, b):
    return jnp.dot(a, b, preferred_element_type=F32)


def kernel(
    nx, nz, nc, cf, vf, cc, vc,
    coarse, row_cond, row_val, col_cond, col_val, near_row, owner_map, near_col,
    out,
    kbuf, work, fbuf, pbuf, smat, ybuf, ysend,
    own_s, enc_s, sel_s,
    ring_recv, ring_send, local_sem, fac_recv, fac_send, facx_recv, facx_send, x_recv, x_send,
):
    me = lax.axis_index("row")
    my_col = lax.axis_index("col")
    my_x, my_z = me // nz, me % nz
    half = nz // 2
    tc, tf = cc * vc, cf * vf
    points = coarse.shape[0] // tc
    shift = points.bit_length() - 1
    assert points == 1 << shift
    fine_rows = out.shape[0] // tf
    width = out.shape[1]
    my_rows = row_cond.shape[0]
    fac_rows = my_rows * cf

    z_up = (my_x * nz + (my_z + 1) % nz, my_col)
    z_down = (my_x * nz + (my_z + nz - 1) % nz, my_col)
    x_peer = [(((my_x + d) % nx) * nz + my_z, my_col) for d in range(nx)]
    col_peer = [(me, (my_col + d) % nc) for d in range(nc)]

    barrier = pltpu.get_barrier_semaphore()
    peers = [z_up, z_down] + x_peer[1:] + col_peer[1:]
    for peer in peers:
        pl.semaphore_signal(barrier, inc=1, device_id=peer, device_id_type=MESH)

    local = pltpu.make_async_copy(coarse, kbuf.at[my_z], local_sem)
    local.start()
    cond = row_cond[...].astype(F32).reshape(fac_rows, cc).astype(BF16)
    val = row_val[...].astype(F32)
    val = jnp.concatenate([val] * (cf // vf), axis=1).reshape(fac_rows, vc).astype(BF16)
    packed = mm(cond, one_hot((cc, 128), lambda k, l: l == k)) + mm(
        val, one_hot((vc, 128), lambda k, l: l == k + cc)
    )
    fbuf[my_x, pl.ds(my_col * fac_rows, fac_rows), :] = packed.astype(BF16)
    pl.semaphore_wait(barrier, len(peers))

    def ring_copy(way, hop, piece, src, first=False):
        rows = pl.ds(piece * tc, tc)
        source = coarse.at[rows, :] if first else kbuf.at[src, rows, :]
        return pltpu.make_async_remote_copy(
            src_ref=source,
            dst_ref=kbuf.at[src, rows, :],
            send_sem=ring_send,
            recv_sem=ring_recv.at[way, hop, piece],
            device_id=z_up if way == 0 else z_down,
            device_id_type=MESH,
        )

    def arrived(way, hop):
        return (my_z + nz - hop) % nz if way == 0 else (my_z + hop) % nz

    for piece in range(points):
        for way in (0, 1):
            ring_copy(way, 1, piece, my_z, first=True).start()

    mine = fbuf.at[my_x, pl.ds(my_col * fac_rows, fac_rows), :]
    for d in range(1, nc):
        pltpu.make_async_remote_copy(
            src_ref=mine, dst_ref=mine, send_sem=fac_send, recv_sem=fac_recv,
            device_id=col_peer[d], device_id_type=MESH,
        ).start()

    def slot_entry(k, carry):
        x, i = k // fine_rows, k % fine_rows
        slot = owner_map[near_row[(x * nz + my_z) * fine_rows + i]]
        own_s[k] = slot >> shift
        enc_s[k] = (i << shift) + (slot & (points - 1))
        return carry

    lax.fori_loop(0, nx * fine_rows, slot_entry, 0)

    others = fbuf.at[my_x, pl.ds(0, (nc - 1) * fac_rows), :]
    fac_all = pltpu.make_async_remote_copy(
        src_ref=others, dst_ref=others, send_sem=fac_send, recv_sem=fac_recv,
        device_id=col_peer[1], device_id_type=MESH,
    )
    fac_all.wait_recv()

    def facx_copy(source_x, d):
        return pltpu.make_async_remote_copy(
            src_ref=fbuf.at[source_x], dst_ref=fbuf.at[source_x], send_sem=facx_send.at[d],
            recv_sem=facx_recv.at[d], device_id=x_peer[d], device_id_type=MESH,
        )

    for d in range(1, nx):
        facx_copy(my_x, d).start()

    def spread_cond(k, l):
        return (k < cc) & (l // vc == k)

    def spread_val(k, l):
        return (k >= cc) & (k < cc + vc) & (l % vc == k - cc)

    def pairs(factors, entries):
        rows = entries * cf
        conds = mm(factors, one_hot((128, tc), spread_cond)).astype(BF16)
        vals = mm(factors, one_hot((128, tc), spread_val)).astype(BF16)
        left = mm(one_hot((entries * tf, rows), lambda t, k: t // vf == k), conds)
        right = mm(
            one_hot((entries * tf, rows), lambda t, k: (t // tf) * cf + t % vf == k), vals
        )
        return left * right

    fine_cols = col_cond.shape[0]
    ccond = col_cond[...].astype(F32).reshape(fine_cols * cf, cc).astype(BF16)
    cval = col_val[...].astype(F32)
    cval = jnp.concatenate([cval] * (cf // vf), axis=1).reshape(fine_cols * cf, vc).astype(BF16)
    cpacked = mm(ccond, one_hot((cc, 128), lambda k, l: l == k)) + mm(
        cval, one_hot((vc, 128), lambda k, l: l == k + cc)
    )
    right_pairs = pairs(cpacked.astype(BF16), fine_cols).T
    lane_point = jnp.zeros((1, width), jnp.int32)
    lane_f = lax.broadcasted_iota(jnp.int32, (1, width), 1) // tf
    for f in range(fine_cols):
        lane_point = jnp.where(lane_f == f, near_col[f], lane_point)
    for c in range(coarse.shape[1] // tc):
        smat[c * tc:(c + 1) * tc, :] = jnp.where(lane_point == c, right_pairs, 0.0).astype(BF16)

    for i in range(fine_rows):
        o = own_s[my_x * fine_rows + i]
        second = jnp.int32(0)
        for k in range(i):
            second = jnp.where(own_s[my_x * fine_rows + k] == o, 1, second)
        sel_s[i] = o * 2 + second

    def finish(z_src):
        o = my_x * nz + z_src
        work[...] = kbuf[z_src].reshape(work.shape)
        parts = []
        for d in range(nx):
            x = (my_x + d) % nx
            first, last = jnp.int32(0), jnp.int32(0)
            hits = []
            for i in range(fine_rows):
                hits.append((own_s[x * fine_rows + i] == o, enc_s[x * fine_rows + i]))
            for i in range(fine_rows):
                last = jnp.where(hits[i][0], hits[i][1], last)
                j = fine_rows - 1 - i
                first = jnp.where(hits[j][0], hits[j][1], first)
            for entry in (first, last):
                parts.append(mm(pbuf[x, entry >> shift], work[entry & (points - 1)]))
        partial = jnp.concatenate(parts, axis=0)
        high = partial.astype(BF16)
        low = (partial - high.astype(F32)).astype(BF16)
        done = (mm(high, smat[...]) + mm(low, smat[...])).astype(BF16)
        done = done.reshape(nx, 2, tf, width)
        ybuf[pl.ds(o * 2, 2)] = done[0]
        for d in range(1, nx):
            ysend[z_src, d - 1] = done[d]
            pltpu.make_async_remote_copy(
                src_ref=ysend.at[z_src, d - 1], dst_ref=ybuf.at[pl.ds(o * 2, 2)], send_sem=x_send,
                recv_sem=x_recv.at[d], device_id=x_peer[d], device_id_type=MESH,
            ).start()

    local.wait()
    for d in range(1, nx):
        facx_copy((my_x + nx - d) % nx, d).wait_recv()
    for x in range(nx):
        pbuf[x] = pairs(fbuf[x], fine_rows).astype(BF16).reshape(fine_rows, tf, tc)
    finish(my_z)

    def hop_step(hop, carry):
        for piece in range(points):
            for way in (0, 1):
                z_src = arrived(way, hop - 1)
                ring_copy(way, hop - 1, piece, z_src).wait_recv()
                ring_copy(way, hop, piece, z_src).start()
        for way in (0, 1):
            finish(arrived(way, hop - 1))
        return carry

    lax.fori_loop(2, half, hop_step, 0)
    for piece in range(points):
        for way in (0, 1):
            z_src = arrived(way, half - 1)
            ring_copy(way, half - 1, piece, z_src).wait_recv()
            if (piece < points // 2) == (way == 0):
                ring_copy(way, half, piece, z_src).start()
    for way in (0, 1):
        finish(arrived(way, half - 1))
    for piece in range(points):
        way = 0 if piece < points // 2 else 1
        ring_copy(way, half, piece, arrived(way, half)).wait_recv()
    finish(arrived(0, half))

    for d in range(1, nx):
        x = (my_x + nx - d) % nx
        block = ybuf.at[pl.ds(x * nz * 2, nz * 2)]
        pltpu.make_async_remote_copy(
            src_ref=block, dst_ref=block, send_sem=x_send, recv_sem=x_recv.at[d],
            device_id=x_peer[d], device_id_type=MESH,
        ).wait_recv()
    for i in range(fine_rows):
        out[i * tf:(i + 1) * tf, :] = ybuf[sel_s[i]]

    ring = kbuf.at[pl.ds(0, nz - 1)]
    pltpu.make_async_remote_copy(
        src_ref=ring, dst_ref=ring, send_sem=ring_send, recv_sem=ring_recv.at[0, 0, 0],
        device_id=z_up, device_id_type=MESH,
    ).wait_send()
    fac_all.wait_send()
    for d in range(1, nx):
        facx_copy(my_x, d).wait_send()
    pltpu.make_async_remote_copy(
        src_ref=ysend, dst_ref=ysend, send_sem=x_send, recv_sem=x_recv.at[0],
        device_id=x_peer[1], device_id_type=MESH,
    ).wait_send()


def shards(nx, nz, nc, coarse, row_cond, row_val, col_cond, col_val, near_row, owner_map, near_col):
    cf, cc = row_cond.shape[1:]
    vf, vc = row_val.shape[1:]
    tc, tf = cc * vc, cf * vf
    points = coarse.shape[0] // tc
    fine_rows = row_cond.shape[0] * nc
    width = col_cond.shape[0] * tf
    span = coarse.shape[1]
    vmem = pl.BlockSpec(memory_space=pltpu.VMEM)
    smem = pl.BlockSpec(memory_space=pltpu.SMEM)
    return pl.pallas_call(
        functools.partial(kernel, nx, nz, nc, cf, vf, cc, vc),
        out_shape=jax.ShapeDtypeStruct((fine_rows * tf, width), BF16),
        in_specs=[pl.BlockSpec(memory_space=pl.ANY), vmem, vmem, vmem, vmem, smem, smem, smem],
        out_specs=vmem,
        scratch_shapes=[
            pltpu.VMEM((nz, points * tc, span), BF16),
            pltpu.VMEM((points, tc, span), BF16),
            pltpu.VMEM((nx, fine_rows * cf, 128), BF16),
            pltpu.VMEM((nx, fine_rows, tf, tc), BF16),
            pltpu.VMEM((span, width), BF16),
            pltpu.VMEM((nx * nz * 2, tf, width), BF16),
            pltpu.VMEM((nz, nx - 1, 2, tf, width), BF16),
            pltpu.SMEM((nx * fine_rows,), jnp.int32),
            pltpu.SMEM((nx * fine_rows,), jnp.int32),
            pltpu.SMEM((fine_rows,), jnp.int32),
            pltpu.SemaphoreType.DMA((2, nz // 2 + 1, points)),
            pltpu.SemaphoreType.DMA,
            pltpu.SemaphoreType.DMA,
            pltpu.SemaphoreType.DMA,
            pltpu.SemaphoreType.DMA,
            pltpu.SemaphoreType.DMA((nx,)),
            pltpu.SemaphoreType.DMA((nx,)),
            pltpu.SemaphoreType.DMA((nx,)),
            pltpu.SemaphoreType.DMA,
        ],
        compiler_params=pltpu.CompilerParams(
            collective_id=0, has_side_effects=True, vmem_limit_bytes=40 * 1024 * 1024
        ),
    )(coarse, row_cond, row_val, col_cond, col_val, near_row, owner_map, near_col)


def solution(mesh, nz=Z_SIZE):
    nx, nc = mesh.shape["row"] // nz, mesh.shape["col"]
    return jax.shard_map(
        functools.partial(shards, nx, nz, nc),
        mesh=mesh,
        in_specs=(
            P("row", "col"),
            P(("row", "col"), None, None),
            P(("row", "col"), None, None),
            P("col", None, None),
            P("col", None, None),
            P(),
            P(),
            P("col"),
        ),
        out_specs=P("row", "col"),
        check_vma=False,
    )
```

time: 415 us -> 73.8 us (0.18)
  waiting for transfers between devices: 338 us -> 0 us
  Pallas kernels: 0 us -> 67 us
  blocking collectives: 25.3 us -> 0 us
  starting transfers between devices: 19.5 us -> 0 us
  local copies, waits for them, and re-layouts: 18.6 us -> 6.45 us
  other arithmetic: 9.97 us -> 0 us
    all_to_all x1 -> x0, waiting for transfers between devices: 338 us -> none  [shards(): lax.all_to_all(outgoing, 'row', split_axis=0, concat_axis=0, tiled=True)]
    pallas_call x0 -> x1, Pallas kernels: none -> 67 us  [shards(): pl.pallas_call(functools.partial(kernel, nx, nz, nc, cf, vf, cc, vc), out...]
    all_gather x2 -> x0, blocking collectives: 25.3 us -> none  [the longest x1 14.1 us: shards(): lax.all_gather(row_cond, 'col', axis=0, tiled=True)]
    all_to_all x1 -> x0, starting transfers between devices: 19.5 us -> none  [shards(): lax.all_to_all(outgoing, 'row', split_axis=0, concat_axis=0, tiled=True)]
    gather x3 -> x0, local copies, waits for them, and re-layouts: 16.4 us -> none  [the longest x1 6.27 us: shards(): outgoing = jnp.take(stored_blocks, wanted, axis=0)]
    select_n x5 -> x0, other arithmetic: 8.13 us -> none  [the longest x2 7.42 us: shards(): outgoing = jnp.take(stored_blocks, wanted, axis=0)]
    unnamed x12 -> x17, local copies, waits for them, and re-layouts: 0.03 us -> 6.45 us
  transfers between devices with their start and end apart: 1 -> 0, of which waited for: 1 -> 0; matrix products, arithmetic and copies ran while one was open for 1% -> 0% of each run, Pallas kernels for 0% -> 0%
where the time goes in v1:
time: 73.8 us; the launch traced here: 73.4 us
  Pallas kernels  67 us (91%)
  local copies, waits for them, and re-layouts  6.45 us (9%)
    pallas_call x1, Pallas kernels, shards(): pl.pallas_call(functools.partial(kernel, nx, nz, nc, cf, vf, cc, vc), out...  67 us
    unnamed x17, local copies, waits for them, and re-layouts  6.45 us

profile of v1, /device:TPU:1, one launch (start us, length us, event | category | flops | bytes accessed | tf_op | source)
XLA Modules:
  0.0 73.4 jit_solution(13154944200578723243)
XLA Ops:
  0.0 0.0 copy-start
  0.0 0.9 %copy-done = bf16[512,256]{1,0:T(8,128)(2,1)S(1)} copy-done((bf16[512,256]{1,0:T(8,128)(2,1)S(1)}, bf16[512,256]{1,0:T(8,128)(2,1)}, u32[]{:S(2)}) %copy-start) | copy-done | bytes 262168
  1.0 0.0 copy-start.1
  1.0 0.7 copy-done.1
  1.7 0.0 copy-start.2
  1.7 0.7 copy-done.2
  2.4 0.0 copy-start.3
  2.4 0.7 copy-done.3
  3.1 0.0 copy-start.4
  3.1 0.7 copy-done.4
  3.7 0.0 copy-start.5
  3.7 0.7 copy-done.5
  4.4 0.0 copy-start.6
  4.4 0.7 copy-done.6
  5.1 0.0 copy-start.7
  5.1 0.7 copy-done.7
  5.8 67.0 %shard_map.82 = bf16[512,256]{1,0:T(8,128)(2,1)S(1)} custom-call(bf16[512,256]{1,0:T(8,128)(2,1)S(1)} %copy-done, bf16[2,8,16]{2,1,0:T(8,128)(2,1)S(1)} %copy-done.3, bf16[2,4,8]{2,1,0:T(4,128)(2,1)S(1)} %copy-done.5, bf16[8,8,16]{2,1,0:T(8,128)(2,1)S(1)} %copy-done.1, bf16[8,4,8]{2,1,0:T(4,128)(2,1)S(1)} %copy-done.2, s32[1024]{0:T(1024)S(1)} %copy-done.4, ...), custom_call_target="tpu_custom_call" | custom-call | tf_op jit(solution)/shard_map/pallas_call | solution.py:251
  72.7 0.7 copy.10
Async XLA Ops:
  0.0 0.9 %copy-start = (bf16[512,256]{1,0:T(8,128)(2,1)S(1)}, bf16[512,256]{1,0:T(8,128)(2,1)}, u32[]{:S(2)}) copy-start(bf16[512,256]{1,0:T(8,128)(2,1)} %coarse.1) | copy-start | bytes 786436
  1.0 0.7 copy-start.1
  1.7 0.7 copy-start.2
  2.4 0.7 copy-start.3
  3.1 0.7 copy-start.4
  3.7 0.7 copy-start.5
  4.4 0.7 copy-start.6
  5.1 0.7 copy-start.7

commit v2 on v1

--- a/solution.py
+++ b/solution.py
@@ -25,11 +25,12 @@
 
 def kernel(
     nx, nz, nc, cf, vf, cc, vc,
-    coarse, row_cond, row_val, col_cond, col_val, near_row, owner_map, near_col,
+    coarse, row_cond_in, row_val_in, col_cond_in, col_val_in, near_row_in, owner_map_in, near_col_in,
     out,
+    row_cond, row_val, col_cond, col_val, near_row, owner_map, near_col,
     kbuf, work, fbuf, pbuf, smat, ybuf, ysend,
     own_s, enc_s, sel_s,
-    ring_recv, ring_send, local_sem, fac_recv, fac_send, facx_recv, facx_send, x_recv, x_send,
+    ring_recv, ring_send, fetch_sem, local_sem, fac_recv, fac_send, facx_recv, facx_send, x_recv, x_send,
 ):
     me = lax.axis_index("row")
     my_col = lax.axis_index("col")
@@ -54,8 +55,20 @@
     for peer in peers:
         pl.semaphore_signal(barrier, inc=1, device_id=peer, device_id_type=MESH)
 
+    fetches = [
+        pltpu.make_async_copy(source, target, fetch_sem.at[k])
+        for k, (source, target) in enumerate((
+            (row_cond_in, row_cond), (row_val_in, row_val), (near_row_in, near_row),
+            (owner_map_in, owner_map), (near_col_in, near_col), (col_cond_in, col_cond),
+            (col_val_in, col_val),
+        ))
+    ]
+    for fetch in fetches:
+        fetch.start()
     local = pltpu.make_async_copy(coarse, kbuf.at[my_z], local_sem)
     local.start()
+    for fetch in fetches[:2]:
+        fetch.wait()
     cond = row_cond[...].astype(F32).reshape(fac_rows, cc).astype(BF16)
     val = row_val[...].astype(F32)
     val = jnp.concatenate([val] * (cf // vf), axis=1).reshape(fac_rows, vc).astype(BF16)
@@ -90,6 +103,9 @@
             src_ref=mine, dst_ref=mine, send_sem=fac_send, recv_sem=fac_recv,
             device_id=col_peer[d], device_id_type=MESH,
         ).start()
+
+    for fetch in fetches[2:]:
+        fetch.wait()
 
     def slot_entry(k, carry):
         x, i = k // fine_rows, k % fine_rows
@@ -246,14 +262,19 @@
     fine_rows = row_cond.shape[0] * nc
     width = col_cond.shape[0] * tf
     span = coarse.shape[1]
-    vmem = pl.BlockSpec(memory_space=pltpu.VMEM)
-    smem = pl.BlockSpec(memory_space=pltpu.SMEM)
     return pl.pallas_call(
         functools.partial(kernel, nx, nz, nc, cf, vf, cc, vc),
         out_shape=jax.ShapeDtypeStruct((fine_rows * tf, width), BF16),
-        in_specs=[pl.BlockSpec(memory_space=pl.ANY), vmem, vmem, vmem, vmem, smem, smem, smem],
-        out_specs=vmem,
+        in_specs=[pl.BlockSpec(memory_space=pltpu.HBM)] * 8,
+        out_specs=pl.BlockSpec(memory_space=pltpu.VMEM),
         scratch_shapes=[
+            pltpu.VMEM(row_cond.shape, BF16),
+            pltpu.VMEM(row_val.shape, BF16),
+            pltpu.VMEM(col_cond.shape, BF16),
+            pltpu.VMEM(col_val.shape, BF16),
+            pltpu.SMEM(near_row.shape, jnp.int32),
+            pltpu.SMEM(owner_map.shape, jnp.int32),
+            pltpu.SMEM(near_col.shape, jnp.int32),
             pltpu.VMEM((nz, points * tc, span), BF16),
             pltpu.VMEM((points, tc, span), BF16),
             pltpu.VMEM((nx, fine_rows * cf, 128), BF16),
@@ -266,6 +287,7 @@
             pltpu.SMEM((fine_rows,), jnp.int32),
             pltpu.SemaphoreType.DMA((2, nz // 2 + 1, points)),
             pltpu.SemaphoreType.DMA,
+            pltpu.SemaphoreType.DMA((7,)),
             pltpu.SemaphoreType.DMA,
             pltpu.SemaphoreType.DMA,
             pltpu.SemaphoreType.DMA,
@@ -275,7 +297,7 @@
             pltpu.SemaphoreType.DMA,
         ],
         compiler_params=pltpu.CompilerParams(
-            collective_id=0, has_side_effects=True, vmem_limit_bytes=40 * 1024 * 1024
+            collective_id=0, has_side_effects=True, vmem_limit_bytes=60 * 1024 * 1024
         ),
     )(coarse, row_cond, row_val, col_cond, col_val, near_row, owner_map, near_col)
 

time: 73.8 us -> 68.9 us (0.934)
  local copies, waits for them, and re-layouts: 6.45 us -> 1.67 us
    unnamed x17 -> x1, local copies, waits for them, and re-layouts: 6.45 us -> 1.67 us
where the time goes in v2:
time: 68.9 us; the launch traced here: 68.8 us
  Pallas kernels  67.1 us (97%)
  local copies, waits for them, and re-layouts  1.67 us (2%)
    pallas_call x1, Pallas kernels, shards(): pl.pallas_call(functools.partial(kernel, nx, nz, nc, cf, vf, cc, vc), out...  67.1 us
    unnamed x1, local copies, waits for them, and re-layouts  1.67 us

profile of v2, /device:TPU:1, one launch (start us, length us, event | category | flops | bytes accessed | tf_op | source)
XLA Modules:
  0.0 68.8 jit_solution(14099535160654049688)
XLA Ops:
  0.0 67.1 %shard_map.82 = bf16[512,256]{1,0:T(8,128)(2,1)} custom-call(bf16[512,256]{1,0:T(8,128)(2,1)} %coarse.1, bf16[2,8,16]{2,1,0:T(8,128)(2,1)} %row_cond_in.1, bf16[2,4,8]{2,1,0:T(4,128)(2,1)} %row_val_in.1, bf16[8,8,16]{2,1,0:T(8,128)(2,1)} %col_cond_in.1, bf16[8,4,8]{2,1,0:T(4,128)(2,1)} %col_val_in.1, s32[1024]{0:T(1024)} %near_row_in.1, s32[256]{0:T(256)} %owner_map_in.1, ...), custom_call_target="tpu_custom_call" | custom-call | tf_op jit(solution)/shard_map/pallas_call | solution.py:265
  67.1 1.7 %copy.10 = bf16[512,256]{1,0:T(8,128)(2,1)} copy(bf16[512,256]{1,0:T(8,128)(2,1)} %shard_map.82) | data formatting | bytes 524288

commit v3 on v2

v3 whole, which is shorter than its diff:
```python
import functools

import jax
import jax.numpy as jnp
from jax import lax
from jax.experimental import pallas as pl
from jax.experimental.pallas import tpu as pltpu
from jax.sharding import PartitionSpec as P

MESH = pl.DeviceIdType.MESH
F32 = jnp.float32
BF16 = jnp.bfloat16
Z_SIZE = 16


def one_hot(shape, test):
    rows = lax.broadcasted_iota(jnp.int32, shape, 0)
    lanes = lax.broadcasted_iota(jnp.int32, shape, 1)
    return jnp.where(test(rows, lanes), 1.0, 0.0).astype(BF16)


def mm(a, b):
    return jnp.dot(a, b, preferred_element_type=F32)


def kernel(
    nx, nz, nc, cf, vf, cc, vc,
    coarse, row_cond_in, row_val_in, col_cond_in, col_val_in, near_row_in, owner_map_in, near_col_in,
    out,
    row_cond, row_val, col_cond, col_val, near_row, owner_map, near_col,
    kbuf, work_0, work_1, fbuf, pbuf, pfar, lane_pat, row_pat, pick, smat, ybuf, ysend, yfar,
    own_s, enc_s, sel_s, found,
    ring_recv, ring_send, fetch_sem, local_sem, fac_recv, fac_send, x_recv, x_send, far_recv, far_send,
):
    me = lax.axis_index("row")
    my_col = lax.axis_index("col")
    my_x, my_z = me // nz, me % nz
    reach = nz // 2 - 2
    near = (-2, -1, 1, 2)
    groups = nx * (1 + len(near))
    tc, tf = cc * vc, cf * vf
    points = coarse.shape[0] // tc
    shift = points.bit_length() - 1
    assert points == 1 << shift
    fine_rows = out.shape[0] // tf
    width = out.shape[1]
    my_rows = row_cond.shape[0]
    row_shift = my_rows.bit_length() - 1
    assert my_rows == 1 << row_shift
    fac_rows = my_rows * cf

    z_up = (my_x * nz + (my_z + 1) % nz, my_col)
    z_down = (my_x * nz + (my_z + nz - 1) % nz, my_col)
    x_peer = [(((my_x + d) % nx) * nz + my_z, my_col) for d in range(nx)]
    col_peer = [(me, (my_col + d) % nc) for d in range(nc)]
    layer_peer = {
        dz: [(((my_x + d) % nx) * nz + (my_z + dz + nz) % nz, my_col) for d in range(nx)]
        for dz in near
    }

    barrier = pltpu.get_barrier_semaphore()
    peers = sum(layer_peer.values(), []) + x_peer[1:] + col_peer[1:]
    for peer in peers:
        pl.semaphore_signal(barrier, inc=1, device_id=peer, device_id_type=MESH)

    fetches = [
        pltpu.make_async_copy(source, target, fetch_sem.at[k])
        for k, (source, target) in enumerate((
            (row_cond_in, row_cond), (row_val_in, row_val), (near_row_in, near_row),
            (owner_map_in, owner_map), (near_col_in, near_col), (col_cond_in, col_cond),
            (col_val_in, col_val),
        ))
    ]
    for fetch in fetches:
        fetch.start()
    local = pltpu.make_async_copy(coarse, kbuf.at[my_z], local_sem)
    local.start()
    pl.semaphore_wait(barrier, len(peers))

    def ring_copy(way, hop, piece, src, first=False):
        rows = pl.ds(piece * tc, tc)
        source = coarse.at[rows, :] if first else kbuf.at[src, rows, :]
        return pltpu.make_async_remote_copy(
            src_ref=source,
            dst_ref=kbuf.at[src, rows, :],
            send_sem=ring_send,
            recv_sem=ring_recv.at[way, hop, piece],
            device_id=z_up if way == 0 else z_down,
            device_id_type=MESH,
        )

    def arrived(way, hop):
        return (my_z + nz - hop) % nz if way == 0 else (my_z + hop) % nz

    for piece in range(points):
        for way in (0, 1):
            ring_copy(way, 1, piece, my_z, first=True).start()

    for fetch in fetches[:2]:
        fetch.wait()
    cond = row_cond[...].astype(F32).reshape(fac_rows, cc).astype(BF16)
    val = row_val[...].astype(F32)
    val = jnp.concatenate([val] * (cf // vf), axis=1).reshape(fac_rows, vc).astype(BF16)
    packed = mm(cond, one_hot((cc, 128), lambda k, l: l == k)) + mm(
        val, one_hot((vc, 128), lambda k, l: l == k + cc)
    )
    fbuf[my_col, my_x] = packed.astype(BF16)
    def move(src, dst, send, recv, peer):
        return pltpu.make_async_remote_copy(
            src_ref=src, dst_ref=dst, send_sem=send, recv_sem=recv, device_id=peer, device_id_type=MESH
        )

    mine = fbuf.at[my_col, my_x]
    for d in range(1, nx):
        move(mine, mine, fac_send, fac_recv.at[0], x_peer[d]).start()
    for dz in near:
        there = fbuf.at[my_col, nx + my_x * len(near) + near.index(-dz)]
        move(mine, there, fac_send, fac_recv.at[1], layer_peer[dz][0]).start()

    def group_place(g):
        far = (g - nx) % len(near)
        dz = far - 2 + jnp.where(far >= 2, 1, 0)
        x = jnp.where(g < nx, g, (g - nx) // len(near))
        return x, (my_z + jnp.where(g < nx, 0, dz) + nz) % nz

    def list_group(g):
        x, z = group_place(g)
        for i in range(fine_rows):
            slot = owner_map[near_row[(x * nz + z) * fine_rows + i]]
            own_s[g * fine_rows + i] = slot >> shift
            enc_s[g * fine_rows + i] = (i << shift) + (slot & (points - 1))

    def list_groups(start, count):
        def one(g, carry):
            list_group(g)
            return carry

        lax.fori_loop(start, start + count, one, 0)

    far_count = nx * len(near)
    layer_tiles = fbuf.at[my_col, pl.ds(0, nx)]
    near_tiles = fbuf.at[my_col, pl.ds(nx + my_x * len(near), len(near))]
    far_tiles = fbuf.at[my_col, pl.ds(nx, far_count)]

    def pass_layer_tiles():
        got = fbuf.at[my_col, pl.ds(0, nx - 1)]
        move(got, got, fac_send, fac_recv.at[0], x_peer[1]).wait_recv()
        for d in range(1, nc):
            move(layer_tiles, layer_tiles, fac_send, fac_recv.at[2], col_peer[d]).start()
        move(near_tiles, near_tiles, fac_send, fac_recv.at[1], z_up).wait_recv()
        for d in range(1, nx):
            move(near_tiles, near_tiles, fac_send, fac_recv.at[3], x_peer[d]).start()

    def pass_far_tiles():
        got = fbuf.at[my_col, pl.ds(nx, far_count - len(near))]
        move(got, got, fac_send, fac_recv.at[3], x_peer[1]).wait_recv()
        for d in range(1, nc):
            move(far_tiles, far_tiles, fac_send, fac_recv.at[4], col_peer[d]).start()

    def make_patterns():
        lane_pat[0] = one_hot((128, tc), lambda k, l: (k < cc) & (l // vc == k))
        lane_pat[1] = one_hot(
            (128, tc), lambda k, l: (k >= cc) & (k < cc + vc) & (l % vc == k - cc)
        )
        shape = row_pat.shape[1:]
        row_pat[0] = one_hot(shape, lambda t, k: t // vf == k)
        row_pat[1] = one_hot(shape, lambda t, k: (t // tf) * cf + t % vf == k)
        for row in range(my_rows):
            pick[row] = one_hot((tf, fac_rows), lambda t, k: k == row * cf + t // vf)
            pick[my_rows + row] = one_hot((tf, fac_rows), lambda t, k: k == row * cf + t % vf)

    def pairs(factors, entries):
        rows = entries * cf
        conds = mm(factors, lane_pat[0]).astype(BF16)
        vals = mm(factors, lane_pat[1]).astype(BF16)
        left = mm(row_pat[0, :entries * tf, :rows], conds)
        return left * mm(row_pat[1, :entries * tf, :rows], vals)

    def make_smat():
        fine_cols = col_cond.shape[0]
        ccond = col_cond[...].astype(F32).reshape(fine_cols * cf, cc).astype(BF16)
        cval = col_val[...].astype(F32)
        cval = jnp.concatenate([cval] * (cf // vf), axis=1)
        cval = cval.reshape(fine_cols * cf, vc).astype(BF16)
        cpacked = mm(ccond, one_hot((cc, 128), lambda k, l: l == k)) + mm(
            cval, one_hot((vc, 128), lambda k, l: l == k + cc)
        )
        right_pairs = pairs(cpacked.astype(BF16), fine_cols).T
        lane_point = jnp.zeros((1, width), jnp.int32)
        lane_f = lax.broadcasted_iota(jnp.int32, (1, width), 1) // tf
        for f in range(fine_cols):
            lane_point = jnp.where(lane_f == f, near_col[f], lane_point)
        for c in range(coarse.shape[1] // tc):
            smat[c * tc:(c + 1) * tc, :] = jnp.where(
                lane_point == c, right_pairs, 0.0
            ).astype(BF16)

    def make_sel():
        for i in range(fine_rows):
            o = own_s[my_x * fine_rows + i]
            second = jnp.int32(0)
            for k in range(i):
                second = jnp.where(own_s[my_x * fine_rows + k] == o, 1, second)
            sel_s[i] = o * 2 + second

    def find(z_src, k, group_of):
        o = my_x * nz + z_src
        for d in range(nx):
            base = group_of((my_x + d) % nx) * fine_rows
            first, last = jnp.int32(0), jnp.int32(0)
            hits = [(own_s[base + i] == o, enc_s[base + i]) for i in range(fine_rows)]
            for i in range(fine_rows):
                last = jnp.where(hits[i][0], hits[i][1], last)
                j = fine_rows - 1 - i
                first = jnp.where(hits[j][0], hits[j][1], first)
            found[k, 2 * d] = first
            found[k, 2 * d + 1] = last

    def rows_of(work, k, d, slots, pair):
        parts = []
        for slot in slots:
            entry = found[k, 2 * d + slot]
            parts.append(mm(pair(entry, slot), work[entry & (points - 1)]))
        partial = parts[0] if len(parts) == 1 else jnp.concatenate(parts, axis=0)
        done = mm(partial.astype(BF16), smat[...]).astype(BF16)
        return done.reshape(len(slots), tf, width)

    def load(work, z_src):
        work[...] = kbuf[z_src].reshape(work.shape)

    works = (work_0, work_1)

    def own_group(x):
        return x

    def finish(work, z_src, k):
        o = my_x * nz + z_src
        for d in [*range(1, nx), 0]:
            group = (my_x + d) % nx
            done = rows_of(work, k, d, (0, 1), lambda entry, slot: pbuf[group, entry >> shift])
            if d == 0:
                ybuf[pl.ds(o * 2, 2)] = done
                continue
            ysend[z_src, d - 1] = done
            move(
                ysend.at[z_src, d - 1], ybuf.at[pl.ds(o * 2, 2)], x_send, x_recv.at[d], x_peer[d]
            ).start()

    def finish_far(work, z_src, k, dz, slots, place):
        o = my_x * nz + z_src
        for d in range(nx):
            at = place + d * len(slots)
            yfar[at:at + len(slots)] = rows_of(
                work, k, d, slots, lambda entry, slot: pfar[at + slot - slots[0]]
            )
            move(
                yfar.at[pl.ds(at, len(slots))], ybuf.at[pl.ds(o * 2 + slots[0], len(slots))],
                far_send, far_recv, layer_peer[dz][d],
            ).start()

    def far_pairs(k, dz, slots, place):
        left, right = [], []
        for d in range(nx):
            group = nx + ((my_x + d) % nx) * len(near) + near.index(dz)
            for slot in slots:
                row = found[k, 2 * d + slot] >> shift
                tile = fbuf[row >> row_shift, group]
                row = row & (my_rows - 1)
                left.append(mm(pick[row], tile).astype(BF16))
                right.append(mm(pick[my_rows + row], tile).astype(BF16))
        product = mm(jnp.concatenate(left, axis=0), lane_pat[0]) * mm(
            jnp.concatenate(right, axis=0), lane_pat[1]
        )
        pfar[place:place + nx * len(slots)] = product.astype(BF16).reshape(-1, tf, tc)

    def forward(hop, piece):
        for way in (0, 1):
            z_src = arrived(way, hop - 1)
            ring_copy(way, hop - 1, piece, z_src).wait_recv()
            ring_copy(way, hop, piece, z_src).start()

    def near_group(dz):
        return lambda x: nx + x * len(near) + near.index(dz)

    def first_lists():
        for fetch in fetches[2:]:
            fetch.wait()
        list_groups(0, nx)
        make_sel()
        find(my_z, 0, own_group)

    def first_matrices():
        make_patterns()
        make_smat()

    beside = [pass_layer_tiles, first_matrices, local.wait]
    first_lists()
    for piece in range(points):
        forward(2, piece)
        if piece < len(beside):
            beside[piece]()
    got = fbuf.at[pl.ds(0, nc - 1), pl.ds(0, nx)]
    move(got, got, fac_send, fac_recv.at[2], col_peer[1]).wait_recv()
    for g in range(nx):
        factors = fbuf[:, g].reshape(nc * fac_rows, 128)
        pbuf[g] = pairs(factors, fine_rows).astype(BF16).reshape(fine_rows, tf, tc)
    load(work_0, my_z)
    finish(work_0, my_z, 0)
    for way in (0, 1):
        find(arrived(way, 1), way, own_group)
    pass_far_tiles()

    share = -(-far_count // (reach - 2))

    def hop_step(hop, carry):
        start = nx + (hop - 3) * share
        count = jnp.minimum(share, groups - start)
        for piece in range(points):
            forward(hop, piece)
            if piece < 2:
                load(works[piece], arrived(piece, hop - 2))
                finish(works[piece], arrived(piece, hop - 2), piece)
            elif piece == 2:
                list_groups(start, count)
        for way in (0, 1):
            find(arrived(way, hop - 1), way, own_group)
        return carry

    lax.fori_loop(3, reach + 1, hop_step, 0)
    for way in (0, 1):
        load(works[way], arrived(way, reach - 1))
        finish(works[way], arrived(way, reach - 1), way)
    got = fbuf.at[pl.ds(0, nc - 1), pl.ds(nx, far_count)]
    move(got, got, fac_send, fac_recv.at[4], col_peer[1]).wait_recv()
    per = nx * 3
    sides = ((0, 1), (1, -1))
    for way, sign in sides:
        z_src = arrived(way, reach)
        find(z_src, 2 + way, near_group(2 * sign))
        find(z_src, 4 + way, near_group(sign))
        far_pairs(2 + way, 2 * sign, (way,), way * per)
        far_pairs(4 + way, sign, (0, 1), way * per + nx)
        find(z_src, way, own_group)
    for way, sign in sides:
        z_src = arrived(way, reach)
        for piece in range(points):
            ring_copy(way, reach, piece, z_src).wait_recv()
        load(works[way], z_src)
        finish_far(works[way], z_src, 2 + way, 2 * sign, (way,), way * per)
        finish_far(works[way], z_src, 4 + way, sign, (0, 1), way * per + nx)
        finish(works[way], z_src, way)

    for d in range(1, nx):
        block = ybuf.at[pl.ds(0, (2 * reach + 1) * 2)]
        move(block, block, x_send, x_recv.at[d], x_peer[d]).wait_recv()
    block = ybuf.at[pl.ds(0, 2 * per)]
    move(block, block, far_send, far_recv, x_peer[1]).wait_recv()
    for i in range(fine_rows):
        out[i * tf:(i + 1) * tf, :] = ybuf[sel_s[i]]

    move(block, block, far_send, far_recv, x_peer[1]).wait_send()
    ring = kbuf.at[pl.ds(0, 2 * reach)]
    move(ring, ring, ring_send, ring_recv.at[0, 0, 0], z_up).wait_send()
    block = ysend.at[pl.ds(0, 2 * reach + 1)]
    move(block, block, x_send, x_recv.at[0], x_peer[1]).wait_send()
    for sent in (
        fbuf.at[0, pl.ds(0, nx - 1)], fbuf.at[0, pl.ds(0, len(near))],
        fbuf.at[pl.ds(0, nc - 1), pl.ds(0, nx)], fbuf.at[pl.ds(0, nx - 1), pl.ds(0, len(near))],
        fbuf.at[pl.ds(0, nc - 1), pl.ds(nx, far_count)],
    ):
        move(sent, sent, fac_send, fac_recv.at[0], x_peer[1]).wait_send()


def shards(nx, nz, nc, coarse, row_cond, row_val, col_cond, col_val, near_row, owner_map, near_col):
    cf, cc = row_cond.shape[1:]
    vf, vc = row_val.shape[1:]
    tc, tf = cc * vc, cf * vf
    points = coarse.shape[0] // tc
    fine_rows = row_cond.shape[0] * nc
    width = col_cond.shape[0] * tf
    groups = nx * 5
    span = coarse.shape[1]
    return pl.pallas_call(
        functools.partial(kernel, nx, nz, nc, cf, vf, cc, vc),
        out_shape=pltpu.VMEM((fine_rows * tf, width), BF16),
        in_specs=[pl.BlockSpec(memory_space=pltpu.HBM)] * 8,
        out_specs=pl.BlockSpec(memory_space=pltpu.VMEM),
        scratch_shapes=[
            pltpu.VMEM(row_cond.shape, BF16),
            pltpu.VMEM(row_val.shape, BF16),
            pltpu.VMEM(col_cond.shape, BF16),
            pltpu.VMEM(col_val.shape, BF16),
            pltpu.SMEM(near_row.shape, jnp.int32),
            pltpu.SMEM(owner_map.shape, jnp.int32),
            pltpu.SMEM(near_col.shape, jnp.int32),
            pltpu.VMEM((nz, points * tc, span), BF16),
            pltpu.VMEM((points, tc, span), BF16),
            pltpu.VMEM((points, tc, span), BF16),
            pltpu.VMEM((nc, groups, row_cond.shape[0] * cf, 128), BF16),
            pltpu.VMEM((nx, fine_rows, tf, tc), BF16),
            pltpu.VMEM((nx * 6, tf, tc), BF16),
            pltpu.VMEM((2, 128, tc), BF16),
            pltpu.VMEM((2, fine_rows * tf, fine_rows * cf), BF16),
            pltpu.VMEM((2 * row_cond.shape[0], tf, row_cond.shape[0] * cf), BF16),
            pltpu.VMEM((span, width), BF16),
            pltpu.VMEM((nx * nz * 2, tf, width), BF16),
            pltpu.VMEM((nz, nx - 1, 2, tf, width), BF16),
            pltpu.VMEM((nx * 6, tf, width), BF16),
            pltpu.SMEM((groups * fine_rows,), jnp.int32),
            pltpu.SMEM((groups * fine_rows,), jnp.int32),
            pltpu.SMEM((fine_rows,), jnp.int32),
            pltpu.SMEM((6, 2 * nx), jnp.int32),
            pltpu.SemaphoreType.DMA((2, nz // 2 + 1, points)),
            pltpu.SemaphoreType.DMA,
            pltpu.SemaphoreType.DMA((7,)),
            pltpu.SemaphoreType.DMA,
            pltpu.SemaphoreType.DMA((5,)),
            pltpu.SemaphoreType.DMA,
            pltpu.SemaphoreType.DMA((nx,)),
            pltpu.SemaphoreType.DMA,
            pltpu.SemaphoreType.DMA,
            pltpu.SemaphoreType.DMA,
        ],
        compiler_params=pltpu.CompilerParams(
            collective_id=0, has_side_effects=True, vmem_limit_bytes=60 * 1024 * 1024
        ),
    )(coarse, row_cond, row_val, col_cond, col_val, near_row, owner_map, near_col)


def solution(mesh, nz=Z_SIZE):
    nx, nc = mesh.shape["row"] // nz, mesh.shape["col"]
    return jax.shard_map(
        functools.partial(shards, nx, nz, nc),
        mesh=mesh,
        in_specs=(
            P("row", "col"),
            P(("row", "col"), None, None),
            P(("row", "col"), None, None),
            P("col", None, None),
            P("col", None, None),
            P(),
            P(),
            P("col"),
        ),
        out_specs=P("row", "col"),
        check_vma=False,
    )
```

time: 68.9 us -> 64.6 us (0.938)
  Pallas kernels: 67.1 us -> 63.8 us
  local copies, waits for them, and re-layouts: 1.67 us -> 0.71 us
    pallas_call x1, Pallas kernels: 67.1 us -> 63.8 us  [shards(): pl.pallas_call(functools.partial(kernel, nx, nz, nc, cf, vf, cc, vc), out...]
    unnamed x1, local copies, waits for them, and re-layouts: 1.67 us -> 0.71 us
where the time goes in v3:
time: 64.6 us; the launch traced here: 64.5 us
  Pallas kernels  63.8 us (99%)
  local copies, waits for them, and re-layouts  0.71 us (1%)
    pallas_call x1, Pallas kernels, shards(): pl.pallas_call(functools.partial(kernel, nx, nz, nc, cf, vf, cc, vc), out...  63.8 us

profile of v3, /device:TPU:1, one launch (start us, length us, event | category | flops | bytes accessed | tf_op | source)
XLA Modules:
  0.0 64.5 jit_solution(969903708361458230)
XLA Ops:
  0.0 63.8 %shard_map.82 = bf16[512,256]{1,0:T(8,128)(2,1)S(1)} custom-call(bf16[512,256]{1,0:T(8,128)(2,1)} %coarse.1, bf16[2,8,16]{2,1,0:T(8,128)(2,1)} %row_cond_in.1, bf16[2,4,8]{2,1,0:T(4,128)(2,1)} %row_val_in.1, bf16[8,8,16]{2,1,0:T(8,128)(2,1)} %col_cond_in.1, bf16[8,4,8]{2,1,0:T(4,128)(2,1)} %col_val_in.1, s32[1024]{0:T(1024)} %near_row_in.1, ...), custom_call_target="tpu_custom_call" | custom-call | tf_op jit(solution)/shard_map/pallas_call | solution.py:383
  63.8 0.7 %copy.10 = bf16[512,256]{1,0:T(8,128)(2,1)} copy(bf16[512,256]{1,0:T(8,128)(2,1)S(1)} %shard_map.82) | data formatting | bytes 524288

commit v4 on v3

--- a/solution.py
+++ b/solution.py
@@ -28,7 +28,7 @@
     coarse, row_cond_in, row_val_in, col_cond_in, col_val_in, near_row_in, owner_map_in, near_col_in,
     out,
     row_cond, row_val, col_cond, col_val, near_row, owner_map, near_col,
-    kbuf, work_0, work_1, fbuf, pbuf, pfar, lane_pat, row_pat, pick, smat, ybuf, ysend, yfar,
+    kbuf, own_left, far_left, fbuf, pbuf, lane_pat, row_pat, pick, smat, ybuf, ysend, yfar,
     own_s, enc_s, sel_s, found,
     ring_recv, ring_send, fetch_sem, local_sem, fac_recv, fac_send, x_recv, x_send, far_recv, far_send,
 ):
@@ -216,62 +216,72 @@
             found[k, 2 * d] = first
             found[k, 2 * d + 1] = last
 
-    def rows_of(work, k, d, slots, pair):
-        parts = []
-        for slot in slots:
-            entry = found[k, 2 * d + slot]
-            parts.append(mm(pair(entry, slot), work[entry & (points - 1)]))
-        partial = parts[0] if len(parts) == 1 else jnp.concatenate(parts, axis=0)
-        done = mm(partial.astype(BF16), smat[...]).astype(BF16)
-        return done.reshape(len(slots), tf, width)
-
-    def load(work, z_src):
-        work[...] = kbuf[z_src].reshape(work.shape)
-
-    works = (work_0, work_1)
-
     def own_group(x):
         return x
 
-    def finish(work, z_src, k):
+    def place_pair(left, way, at, entry, pair):
+        point = entry & (points - 1)
+        for p in range(points):
+            left[way, at * tf:(at + 1) * tf, p * tc:(p + 1) * tc] = jnp.where(point == p, pair, 0)
+
+    def prepare(z_src, way):
+        find(z_src, way, own_group)
+        for d in range(nx):
+            for slot in range(2):
+                entry = found[way, 2 * d + slot]
+                pair = pbuf[(my_x + d) % nx, entry >> shift]
+                place_pair(own_left, way, 2 * d + slot, entry, pair)
+
+    def contract(left, z_src):
+        partial = mm(left, kbuf[z_src]).astype(BF16)
+        return mm(partial, smat[...]).astype(BF16).reshape(-1, tf, width)
+
+    def finish(z_src, way):
         o = my_x * nz + z_src
+        done = contract(own_left[way], z_src)
         for d in [*range(1, nx), 0]:
-            group = (my_x + d) % nx
-            done = rows_of(work, k, d, (0, 1), lambda entry, slot: pbuf[group, entry >> shift])
+            rows = done[2 * d:2 * d + 2]
             if d == 0:
-                ybuf[pl.ds(o * 2, 2)] = done
+                ybuf[pl.ds(o * 2, 2)] = rows
                 continue
-            ysend[z_src, d - 1] = done
+            ysend[z_src, d - 1] = rows
             move(
                 ysend.at[z_src, d - 1], ybuf.at[pl.ds(o * 2, 2)], x_send, x_recv.at[d], x_peer[d]
             ).start()
 
-    def finish_far(work, z_src, k, dz, slots, place):
+    def finish_far(z_src, way, sign):
         o = my_x * nz + z_src
-        for d in range(nx):
-            at = place + d * len(slots)
-            yfar[at:at + len(slots)] = rows_of(
-                work, k, d, slots, lambda entry, slot: pfar[at + slot - slots[0]]
-            )
-            move(
-                yfar.at[pl.ds(at, len(slots))], ybuf.at[pl.ds(o * 2 + slots[0], len(slots))],
-                far_send, far_recv, layer_peer[dz][d],
-            ).start()
-
-    def far_pairs(k, dz, slots, place):
-        left, right = [], []
-        for d in range(nx):
-            group = nx + ((my_x + d) % nx) * len(near) + near.index(dz)
-            for slot in slots:
-                row = found[k, 2 * d + slot] >> shift
-                tile = fbuf[row >> row_shift, group]
-                row = row & (my_rows - 1)
-                left.append(mm(pick[row], tile).astype(BF16))
-                right.append(mm(pick[my_rows + row], tile).astype(BF16))
+        place = way * nx * 3
+        yfar[place:place + nx * 3] = contract(far_left[way], z_src)
+        for dz, slots, at in ((2 * sign, (way,), place), (sign, (0, 1), place + nx)):
+            for d in range(nx):
+                move(
+                    yfar.at[pl.ds(at + d * len(slots), len(slots))],
+                    ybuf.at[pl.ds(o * 2 + slots[0], len(slots))],
+                    far_send, far_recv, layer_peer[dz][d],
+                ).start()
+
+    def prepare_far(way, sign):
+        left, right, entries = [], [], []
+        z_src = arrived(way, reach)
+        for k, dz, slots in ((2, 2 * sign, (way,)), (3, sign, (0, 1))):
+            find(z_src, k, lambda x: nx + x * len(near) + near.index(dz))
+            for d in range(nx):
+                group = nx + ((my_x + d) % nx) * len(near) + near.index(dz)
+                for slot in slots:
+                    entry = found[k, 2 * d + slot]
+                    row = entry >> shift
+                    tile = fbuf[row >> row_shift, group]
+                    row = row & (my_rows - 1)
+                    entries.append(entry)
+                    left.append(mm(pick[row], tile).astype(BF16))
+                    right.append(mm(pick[my_rows + row], tile).astype(BF16))
         product = mm(jnp.concatenate(left, axis=0), lane_pat[0]) * mm(
             jnp.concatenate(right, axis=0), lane_pat[1]
         )
-        pfar[place:place + nx * len(slots)] = product.astype(BF16).reshape(-1, tf, tc)
+        product = product.astype(BF16)
+        for at, entry in enumerate(entries):
+            place_pair(far_left, way, at, entry, product[at * tf:(at + 1) * tf])
 
     def forward(hop, piece):
         for way in (0, 1):
@@ -279,15 +289,11 @@
             ring_copy(way, hop - 1, piece, z_src).wait_recv()
             ring_copy(way, hop, piece, z_src).start()
 
-    def near_group(dz):
-        return lambda x: nx + x * len(near) + near.index(dz)
-
     def first_lists():
         for fetch in fetches[2:]:
             fetch.wait()
         list_groups(0, nx)
         make_sel()
-        find(my_z, 0, own_group)
 
     def first_matrices():
         make_patterns()
@@ -304,10 +310,10 @@
     for g in range(nx):
         factors = fbuf[:, g].reshape(nc * fac_rows, 128)
         pbuf[g] = pairs(factors, fine_rows).astype(BF16).reshape(fine_rows, tf, tc)
-    load(work_0, my_z)
-    finish(work_0, my_z, 0)
+    prepare(my_z, 0)
+    finish(my_z, 0)
     for way in (0, 1):
-        find(arrived(way, 1), way, own_group)
+        prepare(arrived(way, 1), way)
     pass_far_tiles()
 
     share = -(-far_count // (reach - 2))
@@ -318,42 +324,33 @@
         for piece in range(points):
             forward(hop, piece)
             if piece < 2:
-                load(works[piece], arrived(piece, hop - 2))
-                finish(works[piece], arrived(piece, hop - 2), piece)
+                finish(arrived(piece, hop - 2), piece)
             elif piece == 2:
                 list_groups(start, count)
         for way in (0, 1):
-            find(arrived(way, hop - 1), way, own_group)
+            prepare(arrived(way, hop - 1), way)
         return carry
 
     lax.fori_loop(3, reach + 1, hop_step, 0)
     for way in (0, 1):
-        load(works[way], arrived(way, reach - 1))
-        finish(works[way], arrived(way, reach - 1), way)
+        finish(arrived(way, reach - 1), way)
     got = fbuf.at[pl.ds(0, nc - 1), pl.ds(nx, far_count)]
     move(got, got, fac_send, fac_recv.at[4], col_peer[1]).wait_recv()
-    per = nx * 3
     sides = ((0, 1), (1, -1))
     for way, sign in sides:
-        z_src = arrived(way, reach)
-        find(z_src, 2 + way, near_group(2 * sign))
-        find(z_src, 4 + way, near_group(sign))
-        far_pairs(2 + way, 2 * sign, (way,), way * per)
-        far_pairs(4 + way, sign, (0, 1), way * per + nx)
-        find(z_src, way, own_group)
+        prepare_far(way, sign)
+        prepare(arrived(way, reach), way)
     for way, sign in sides:
         z_src = arrived(way, reach)
         for piece in range(points):
             ring_copy(way, reach, piece, z_src).wait_recv()
-        load(works[way], z_src)
-        finish_far(works[way], z_src, 2 + way, 2 * sign, (way,), way * per)
-        finish_far(works[way], z_src, 4 + way, sign, (0, 1), way * per + nx)
-        finish(works[way], z_src, way)
+        finish_far(z_src, way, sign)
+        finish(z_src, way)
 
     for d in range(1, nx):
         block = ybuf.at[pl.ds(0, (2 * reach + 1) * 2)]
         move(block, block, x_send, x_recv.at[d], x_peer[d]).wait_recv()
-    block = ybuf.at[pl.ds(0, 2 * per)]
+    block = ybuf.at[pl.ds(0, nx * 6)]
     move(block, block, far_send, far_recv, x_peer[1]).wait_recv()
     for i in range(fine_rows):
         out[i * tf:(i + 1) * tf, :] = ybuf[sel_s[i]]
@@ -394,11 +391,10 @@
             pltpu.SMEM(owner_map.shape, jnp.int32),
             pltpu.SMEM(near_col.shape, jnp.int32),
             pltpu.VMEM((nz, points * tc, span), BF16),
-            pltpu.VMEM((points, tc, span), BF16),
-            pltpu.VMEM((points, tc, span), BF16),
+            pltpu.VMEM((2, nx * 2 * tf, points * tc), BF16),
+            pltpu.VMEM((2, nx * 3 * tf, points * tc), BF16),
             pltpu.VMEM((nc, groups, row_cond.shape[0] * cf, 128), BF16),
             pltpu.VMEM((nx, fine_rows, tf, tc), BF16),
-            pltpu.VMEM((nx * 6, tf, tc), BF16),
             pltpu.VMEM((2, 128, tc), BF16),
             pltpu.VMEM((2, fine_rows * tf, fine_rows * cf), BF16),
             pltpu.VMEM((2 * row_cond.shape[0], tf, row_cond.shape[0] * cf), BF16),
@@ -409,7 +405,7 @@
             pltpu.SMEM((groups * fine_rows,), jnp.int32),
             pltpu.SMEM((groups * fine_rows,), jnp.int32),
             pltpu.SMEM((fine_rows,), jnp.int32),
-            pltpu.SMEM((6, 2 * nx), jnp.int32),
+            pltpu.SMEM((4, 2 * nx), jnp.int32),
             pltpu.SemaphoreType.DMA((2, nz // 2 + 1, points)),
             pltpu.SemaphoreType.DMA,
             pltpu.SemaphoreType.DMA((7,)),

time: 64.6 us -> 61.6 us (0.954)
  Pallas kernels: 63.8 us -> 60.8 us
    pallas_call x1, Pallas kernels: 63.8 us -> 60.8 us  [shards(): pl.pallas_call(functools.partial(kernel, nx, nz, nc, cf, vf, cc, vc), out...]
where the time goes in v4:
time: 61.6 us; the launch traced here: 61.5 us
  Pallas kernels  60.8 us (99%)
  local copies, waits for them, and re-layouts  0.71 us (1%)
    pallas_call x1, Pallas kernels, shards(): pl.pallas_call(functools.partial(kernel, nx, nz, nc, cf, vf, cc, vc), out...  60.8 us

profile of v4, /device:TPU:1, one launch (start us, length us, event | category | flops | bytes accessed | tf_op | source)
XLA Modules:
  0.0 61.5 jit_solution(14472180116510635636)
XLA Ops:
  0.0 60.8 %shard_map.82 = bf16[512,256]{1,0:T(8,128)(2,1)S(1)} custom-call(bf16[512,256]{1,0:T(8,128)(2,1)} %coarse.1, bf16[2,8,16]{2,1,0:T(8,128)(2,1)} %row_cond_in.1, bf16[2,4,8]{2,1,0:T(4,128)(2,1)} %row_val_in.1, bf16[8,8,16]{2,1,0:T(8,128)(2,1)} %col_cond_in.1, bf16[8,4,8]{2,1,0:T(4,128)(2,1)} %col_val_in.1, s32[1024]{0:T(1024)} %near_row_in.1, ...), custom_call_target="tpu_custom_call" | custom-call | tf_op jit(solution)/shard_map/pallas_call | solution.py:380
  60.8 0.7 %copy.10 = bf16[512,256]{1,0:T(8,128)(2,1)} copy(bf16[512,256]{1,0:T(8,128)(2,1)S(1)} %shard_map.82) | data formatting | bytes 524288

commit v5 on v4

--- a/solution.py
+++ b/solution.py
@@ -30,7 +30,7 @@
     row_cond, row_val, col_cond, col_val, near_row, owner_map, near_col,
     kbuf, own_left, far_left, fbuf, pbuf, lane_pat, row_pat, pick, smat, ybuf, ysend, yfar,
     own_s, enc_s, sel_s, found,
-    ring_recv, ring_send, fetch_sem, local_sem, fac_recv, fac_send, x_recv, x_send, far_recv, far_send,
+    ready, ring_recv, ring_send, fetch_sem, local_sem, fac_recv, fac_send, x_recv, x_send, far_recv, far_send,
 ):
     me = lax.axis_index("row")
     my_col = lax.axis_index("col")
@@ -59,9 +59,42 @@
     }
 
     barrier = pltpu.get_barrier_semaphore()
-    peers = sum(layer_peer.values(), []) + x_peer[1:] + col_peer[1:]
-    for peer in peers:
-        pl.semaphore_signal(barrier, inc=1, device_id=peer, device_id_type=MESH)
+
+    def greet(semaphore, peer):
+        pl.semaphore_signal(semaphore, inc=1, device_id=peer, device_id_type=MESH)
+
+    def greet_peers(semaphore, higher):
+        def x_one(x, carry):
+            greet(semaphore, (x * nz + my_z, my_col))
+            return carry
+
+        def col_one(col, carry):
+            greet(semaphore, (me, col))
+            return carry
+
+        if higher:
+            lax.fori_loop(my_x + 1, nx, x_one, 0)
+            lax.fori_loop(my_col + 1, nc, col_one, 0)
+        else:
+            lax.fori_loop(0, my_x, x_one, 0)
+            lax.fori_loop(0, my_col, col_one, 0)
+        for dz in near:
+            z = (my_z + dz + nz) % nz
+            planes = layer_peer[dz][1:] if abs(dz) == 1 else layer_peer[dz]
+
+            @pl.when(z > my_z if higher else z < my_z)
+            def _():
+                for peer in planes:
+                    greet(semaphore, peer)
+
+    lower, count_all = my_x + my_col, nx - 1 + nc - 1
+    for dz in near:
+        planes = nx - 1 if abs(dz) == 1 else nx
+        lower = lower + jnp.where((my_z + dz + nz) % nz < my_z, planes, 0)
+        count_all += planes
+    greet(barrier, z_up)
+    greet(barrier, z_down)
+    greet_peers(barrier, True)
 
     fetches = [
         pltpu.make_async_copy(source, target, fetch_sem.at[k])
@@ -75,7 +108,7 @@
         fetch.start()
     local = pltpu.make_async_copy(coarse, kbuf.at[my_z], local_sem)
     local.start()
-    pl.semaphore_wait(barrier, len(peers))
+    pl.semaphore_wait(barrier, 2 + lower)
 
     def ring_copy(way, hop, piece, src, first=False):
         rows = pl.ds(piece * tc, tc)
@@ -98,6 +131,7 @@
 
     for fetch in fetches[:2]:
         fetch.wait()
+    greet_peers(ready, False)
     cond = row_cond[...].astype(F32).reshape(fac_rows, cc).astype(BF16)
     val = row_val[...].astype(F32)
     val = jnp.concatenate([val] * (cf // vf), axis=1).reshape(fac_rows, vc).astype(BF16)
@@ -110,12 +144,17 @@
             src_ref=src, dst_ref=dst, send_sem=send, recv_sem=recv, device_id=peer, device_id_type=MESH
         )
 
-    mine = fbuf.at[my_col, my_x]
-    for d in range(1, nx):
-        move(mine, mine, fac_send, fac_recv.at[0], x_peer[d]).start()
-    for dz in near:
-        there = fbuf.at[my_col, nx + my_x * len(near) + near.index(-dz)]
-        move(mine, there, fac_send, fac_recv.at[1], layer_peer[dz][0]).start()
+    def send_tiles():
+        @pl.when(count_all > lower)
+        def _():
+            pl.semaphore_wait(ready, count_all - lower)
+
+        mine = fbuf.at[my_col, my_x]
+        for d in range(1, nx):
+            move(mine, mine, fac_send, fac_recv.at[0], x_peer[d]).start()
+        for dz in near:
+            there = fbuf.at[my_col, nx + my_x * len(near) + near.index(-dz)]
+            move(mine, there, fac_send, fac_recv.at[1], layer_peer[dz][0]).start()
 
     def group_place(g):
         far = (g - nx) % len(near)
@@ -295,45 +334,38 @@
         list_groups(0, nx)
         make_sel()
 
-    def first_matrices():
-        make_patterns()
-        make_smat()
-
-    beside = [pass_layer_tiles, first_matrices, local.wait]
-    first_lists()
-    for piece in range(points):
-        forward(2, piece)
-        if piece < len(beside):
-            beside[piece]()
-    got = fbuf.at[pl.ds(0, nc - 1), pl.ds(0, nx)]
-    move(got, got, fac_send, fac_recv.at[2], col_peer[1]).wait_recv()
-    for g in range(nx):
-        factors = fbuf[:, g].reshape(nc * fac_rows, 128)
-        pbuf[g] = pairs(factors, fine_rows).astype(BF16).reshape(fine_rows, tf, tc)
-    prepare(my_z, 0)
-    finish(my_z, 0)
-    for way in (0, 1):
-        prepare(arrived(way, 1), way)
-    pass_far_tiles()
-
-    share = -(-far_count // (reach - 2))
-
-    def hop_step(hop, carry):
-        start = nx + (hop - 3) * share
-        count = jnp.minimum(share, groups - start)
+    def make_pairs():
+        got = fbuf.at[pl.ds(0, nc - 1), pl.ds(0, nx)]
+        move(got, got, fac_send, fac_recv.at[2], col_peer[1]).wait_recv()
+        for g in range(nx):
+            factors = fbuf[:, g].reshape(nc * fac_rows, 128)
+            pbuf[g] = pairs(factors, fine_rows).astype(BF16).reshape(fine_rows, tf, tc)
+
+    def finish_chunk(hop, way):
+        def task():
+            z_src = arrived(way, hop)
+            prepare(z_src, way)
+            finish(z_src, way)
+
+        return task
+
+    share = far_count // 4
+
+    def near_lists(k):
+        return lambda: list_groups(nx + k * share, share)
+
+    tasks = [first_lists, send_tiles, make_patterns, make_smat]
+    tasks += [pass_layer_tiles, near_lists(0), pass_far_tiles, make_pairs]
+    chunks = [finish_chunk(hop, way) for hop in range(1, reach) for way in (0, 1)]
+    tasks += [finish_chunk(0, 0)] + chunks[:6] + [near_lists(1)] + chunks[6:8]
+    tasks += [near_lists(2), near_lists(3)] + chunks[8:]
+    local.wait()
+    for hop in range(2, reach + 1):
         for piece in range(points):
             forward(hop, piece)
-            if piece < 2:
-                finish(arrived(piece, hop - 2), piece)
-            elif piece == 2:
-                list_groups(start, count)
-        for way in (0, 1):
-            prepare(arrived(way, hop - 1), way)
-        return carry
-
-    lax.fori_loop(3, reach + 1, hop_step, 0)
-    for way in (0, 1):
-        finish(arrived(way, reach - 1), way)
+            tasks.pop(0)()
+    for task in tasks:
+        task()
     got = fbuf.at[pl.ds(0, nc - 1), pl.ds(nx, far_count)]
     move(got, got, fac_send, fac_recv.at[4], col_peer[1]).wait_recv()
     sides = ((0, 1), (1, -1))
@@ -406,6 +438,7 @@
             pltpu.SMEM((groups * fine_rows,), jnp.int32),
             pltpu.SMEM((fine_rows,), jnp.int32),
             pltpu.SMEM((4, 2 * nx), jnp.int32),
+            pltpu.SemaphoreType.REGULAR,
             pltpu.SemaphoreType.DMA((2, nz // 2 + 1, points)),
             pltpu.SemaphoreType.DMA,
             pltpu.SemaphoreType.DMA((7,)),

time: 61.6 us -> 59.6 us (0.968)
  Pallas kernels: 60.8 us -> 58.7 us
    pallas_call x1, Pallas kernels: 60.8 us -> 58.7 us  [shards(): pl.pallas_call(functools.partial(kernel, nx, nz, nc, cf, vf, cc, vc), out...]
where the time goes in v5:
time: 59.6 us; the launch traced here: 59.5 us
  Pallas kernels  58.7 us (98%)
  local copies, waits for them, and re-layouts  0.71 us (1%)
    pallas_call x1, Pallas kernels, shards(): pl.pallas_call(functools.partial(kernel, nx, nz, nc, cf, vf, cc, vc), out...  58.7 us

profile of v5, /device:TPU:1, one launch (start us, length us, event | category | flops | bytes accessed | tf_op | source)
XLA Modules:
  0.0 59.5 jit_solution(17992626177674855947)
XLA Ops:
  0.0 58.7 %shard_map.82 = bf16[512,256]{1,0:T(8,128)(2,1)S(1)} custom-call(bf16[512,256]{1,0:T(8,128)(2,1)} %coarse.1, bf16[2,8,16]{2,1,0:T(8,128)(2,1)} %row_cond_in.1, bf16[2,4,8]{2,1,0:T(4,128)(2,1)} %row_val_in.1, bf16[8,8,16]{2,1,0:T(8,128)(2,1)} %col_cond_in.1, bf16[8,4,8]{2,1,0:T(4,128)(2,1)} %col_val_in.1, s32[1024]{0:T(1024)} %near_row_in.1, ...), custom_call_target="tpu_custom_call" | custom-call | tf_op jit(solution)/shard_map/pallas_call | solution.py:412
  58.7 0.7 %copy.10 = bf16[512,256]{1,0:T(8,128)(2,1)} copy(bf16[512,256]{1,0:T(8,128)(2,1)S(1)} %shard_map.82) | data formatting | bytes 524288

commit v6 on v5

--- a/solution.py
+++ b/solution.py
@@ -28,7 +28,7 @@
     coarse, row_cond_in, row_val_in, col_cond_in, col_val_in, near_row_in, owner_map_in, near_col_in,
     out,
     row_cond, row_val, col_cond, col_val, near_row, owner_map, near_col,
-    kbuf, own_left, far_left, fbuf, pbuf, lane_pat, row_pat, pick, smat, ybuf, ysend, yfar,
+    kbuf, own_left, far_left, fbuf, pbuf, lane_pat, row_pat, pick, smat, ybuf, ysend, yfar, ysel,
     own_s, enc_s, sel_s, found,
     ready, ring_recv, ring_send, fetch_sem, local_sem, fac_recv, fac_send, x_recv, x_send, far_recv, far_send,
 ):
@@ -48,6 +48,7 @@
     row_shift = my_rows.bit_length() - 1
     assert my_rows == 1 << row_shift
     fac_rows = my_rows * cf
+    lanes, block_rows = coarse.shape[1] // 2, coarse.shape[0] // 2
 
     z_up = (my_x * nz + (my_z + 1) % nz, my_col)
     z_down = (my_x * nz + (my_z + nz - 1) % nz, my_col)
@@ -106,16 +107,23 @@
     ]
     for fetch in fetches:
         fetch.start()
-    local = pltpu.make_async_copy(coarse, kbuf.at[my_z], local_sem)
-    local.start()
+    locals_ = [
+        pltpu.make_async_copy(
+            coarse.at[:, pl.ds(part * lanes, lanes)], kbuf.at[my_z, part], local_sem.at[part]
+        )
+        for part in (0, 1)
+    ]
+    for local in locals_:
+        local.start()
     pl.semaphore_wait(barrier, 2 + lower)
 
     def ring_copy(way, hop, piece, src, first=False):
-        rows = pl.ds(piece * tc, tc)
-        source = coarse.at[rows, :] if first else kbuf.at[src, rows, :]
+        part, rows = piece // 2, pl.ds((piece % 2) * block_rows, block_rows)
+        target = kbuf.at[src, part, rows, :]
+        source = coarse.at[rows, pl.ds(part * lanes, lanes)] if first else target
         return pltpu.make_async_remote_copy(
             src_ref=source,
-            dst_ref=kbuf.at[src, rows, :],
+            dst_ref=target,
             send_sem=ring_send,
             recv_sem=ring_recv.at[way, hop, piece],
             device_id=z_up if way == 0 else z_down,
@@ -271,32 +279,35 @@
                 pair = pbuf[(my_x + d) % nx, entry >> shift]
                 place_pair(own_left, way, 2 * d + slot, entry, pair)
 
-    def contract(left, z_src):
-        partial = mm(left, kbuf[z_src]).astype(BF16)
-        return mm(partial, smat[...]).astype(BF16).reshape(-1, tf, width)
-
-    def finish(z_src, way):
+    def contract(left, z_src, part):
+        return mm(left, kbuf[z_src, part]).astype(BF16).reshape(-1, tf, lanes)
+
+    def finish(z_src, way, parts=(0, 1)):
         o = my_x * nz + z_src
-        done = contract(own_left[way], z_src)
+        done = [contract(own_left[way], z_src, part) for part in parts]
         for d in [*range(1, nx), 0]:
-            rows = done[2 * d:2 * d + 2]
+            for part, rows in zip(parts, done):
+                if d == 0:
+                    ybuf[part, pl.ds(o * 2, 2)] = rows[:2]
+                else:
+                    ysend[z_src, d - 1, part] = rows[2 * d:2 * d + 2]
             if d == 0:
-                ybuf[pl.ds(o * 2, 2)] = rows
                 continue
-            ysend[z_src, d - 1] = rows
+            span = pl.ds(parts[0], len(parts))
             move(
-                ysend.at[z_src, d - 1], ybuf.at[pl.ds(o * 2, 2)], x_send, x_recv.at[d], x_peer[d]
+                ysend.at[z_src, d - 1, span], ybuf.at[span, pl.ds(o * 2, 2)],
+                x_send, x_recv.at[d], x_peer[d],
             ).start()
 
-    def finish_far(z_src, way, sign):
+    def finish_far(z_src, way, sign, part):
         o = my_x * nz + z_src
         place = way * nx * 3
-        yfar[place:place + nx * 3] = contract(far_left[way], z_src)
+        yfar[part, place:place + nx * 3] = contract(far_left[way], z_src, part)
         for dz, slots, at in ((2 * sign, (way,), place), (sign, (0, 1), place + nx)):
             for d in range(nx):
                 move(
-                    yfar.at[pl.ds(at + d * len(slots), len(slots))],
-                    ybuf.at[pl.ds(o * 2 + slots[0], len(slots))],
+                    yfar.at[part, pl.ds(at + d * len(slots), len(slots))],
+                    ybuf.at[part, pl.ds(o * 2 + slots[0], len(slots))],
                     far_send, far_recv, layer_peer[dz][d],
                 ).start()
 
@@ -354,38 +365,54 @@
     def near_lists(k):
         return lambda: list_groups(nx + k * share, share)
 
+    def pass_far_and_list():
+        pass_far_tiles()
+        list_groups(nx + share, share)
+
+    def prepare_both(hop):
+        for way in (0, 1):
+            prepare(arrived(way, hop), way)
+
+    def list_last():
+        list_groups(nx + 3 * share, share)
+        prepare_both(reach - 1)
+
+    chunks = [finish_chunk(hop, way) for hop in range(1, reach - 1) for way in (0, 1)]
     tasks = [first_lists, send_tiles, make_patterns, make_smat]
-    tasks += [pass_layer_tiles, near_lists(0), pass_far_tiles, make_pairs]
-    chunks = [finish_chunk(hop, way) for hop in range(1, reach) for way in (0, 1)]
-    tasks += [finish_chunk(0, 0)] + chunks[:6] + [near_lists(1)] + chunks[6:8]
-    tasks += [near_lists(2), near_lists(3)] + chunks[8:]
-    local.wait()
+    tasks += [pass_layer_tiles, near_lists(0), pass_far_and_list, make_pairs]
+    tasks += [finish_chunk(0, 0)] + chunks[:6] + [near_lists(2)] + chunks[6:] + [list_last]
+    for local in locals_:
+        local.wait()
     for hop in range(2, reach + 1):
         for piece in range(points):
             forward(hop, piece)
-            tasks.pop(0)()
-    for task in tasks:
-        task()
+            if tasks:
+                tasks.pop(0)()
+    for way in (0, 1):
+        finish(arrived(way, reach - 1), way)
     got = fbuf.at[pl.ds(0, nc - 1), pl.ds(nx, far_count)]
     move(got, got, fac_send, fac_recv.at[4], col_peer[1]).wait_recv()
     sides = ((0, 1), (1, -1))
     for way, sign in sides:
         prepare_far(way, sign)
         prepare(arrived(way, reach), way)
-    for way, sign in sides:
-        z_src = arrived(way, reach)
-        for piece in range(points):
-            ring_copy(way, reach, piece, z_src).wait_recv()
-        finish_far(z_src, way, sign)
-        finish(z_src, way)
+    for part in (0, 1):
+        for way, sign in sides:
+            z_src = arrived(way, reach)
+            for piece in (2 * part, 2 * part + 1):
+                ring_copy(way, reach, piece, z_src).wait_recv()
+            finish_far(z_src, way, sign, part)
+            finish(z_src, way, (part,))
 
     for d in range(1, nx):
-        block = ybuf.at[pl.ds(0, (2 * reach + 1) * 2)]
+        block = ybuf.at[:, pl.ds(0, (2 * reach + 1) * 2)]
         move(block, block, x_send, x_recv.at[d], x_peer[d]).wait_recv()
-    block = ybuf.at[pl.ds(0, nx * 6)]
+    block = ybuf.at[:, pl.ds(0, nx * 6)]
     move(block, block, far_send, far_recv, x_peer[1]).wait_recv()
     for i in range(fine_rows):
-        out[i * tf:(i + 1) * tf, :] = ybuf[sel_s[i]]
+        for part in (0, 1):
+            ysel[i * tf:(i + 1) * tf, part * lanes:(part + 1) * lanes] = ybuf[part, sel_s[i]]
+    out[...] = mm(ysel[...], smat[...]).astype(BF16)
 
     move(block, block, far_send, far_recv, x_peer[1]).wait_send()
     ring = kbuf.at[pl.ds(0, 2 * reach)]
@@ -422,7 +449,7 @@
             pltpu.SMEM(near_row.shape, jnp.int32),
             pltpu.SMEM(owner_map.shape, jnp.int32),
             pltpu.SMEM(near_col.shape, jnp.int32),
-            pltpu.VMEM((nz, points * tc, span), BF16),
+            pltpu.VMEM((nz, 2, points * tc, span // 2), BF16),
             pltpu.VMEM((2, nx * 2 * tf, points * tc), BF16),
             pltpu.VMEM((2, nx * 3 * tf, points * tc), BF16),
             pltpu.VMEM((nc, groups, row_cond.shape[0] * cf, 128), BF16),
@@ -431,9 +458,10 @@
             pltpu.VMEM((2, fine_rows * tf, fine_rows * cf), BF16),
             pltpu.VMEM((2 * row_cond.shape[0], tf, row_cond.shape[0] * cf), BF16),
             pltpu.VMEM((span, width), BF16),
-            pltpu.VMEM((nx * nz * 2, tf, width), BF16),
-            pltpu.VMEM((nz, nx - 1, 2, tf, width), BF16),
-            pltpu.VMEM((nx * 6, tf, width), BF16),
+            pltpu.VMEM((2, nx * nz * 2, tf, span // 2), BF16),
+            pltpu.VMEM((nz, nx - 1, 2, 2, tf, span // 2), BF16),
+            pltpu.VMEM((2, nx * 6, tf, span // 2), BF16),
+            pltpu.VMEM((fine_rows * tf, span), BF16),
             pltpu.SMEM((groups * fine_rows,), jnp.int32),
             pltpu.SMEM((groups * fine_rows,), jnp.int32),
             pltpu.SMEM((fine_rows,), jnp.int32),
@@ -442,7 +470,7 @@
             pltpu.SemaphoreType.DMA((2, nz // 2 + 1, points)),
             pltpu.SemaphoreType.DMA,
             pltpu.SemaphoreType.DMA((7,)),
-            pltpu.SemaphoreType.DMA,
+            pltpu.SemaphoreType.DMA((2,)),
             pltpu.SemaphoreType.DMA((5,)),
             pltpu.SemaphoreType.DMA,
             pltpu.SemaphoreType.DMA((nx,)),

time: 59.6 us -> 58.3 us (0.978); the launches traced: 59.5 us -> 57.5 us
  Pallas kernels: 58.7 us -> 56.8 us
    pallas_call x1, Pallas kernels: 58.7 us -> 56.8 us  [shards(): pl.pallas_call(functools.partial(kernel, nx, nz, nc, cf, vf, cc, vc), out...]
where the time goes in v6:
time: 58.3 us; the launch traced here: 57.5 us
  Pallas kernels  56.8 us (97%)
  local copies, waits for them, and re-layouts  0.71 us (1%)
    pallas_call x1, Pallas kernels, shards(): pl.pallas_call(functools.partial(kernel, nx, nz, nc, cf, vf, cc, vc), out...  56.8 us

profile of v6, /device:TPU:1, one launch (start us, length us, event | category | flops | bytes accessed | tf_op | source)
XLA Modules:
  0.0 57.5 jit_solution(1967220647606309562)
XLA Ops:
  0.0 56.8 %shard_map.82 = bf16[512,256]{1,0:T(8,128)(2,1)S(1)} custom-call(bf16[512,256]{1,0:T(8,128)(2,1)} %coarse.1, bf16[2,8,16]{2,1,0:T(8,128)(2,1)} %row_cond_in.1, bf16[2,4,8]{2,1,0:T(4,128)(2,1)} %row_val_in.1, bf16[8,8,16]{2,1,0:T(8,128)(2,1)} %col_cond_in.1, bf16[8,4,8]{2,1,0:T(4,128)(2,1)} %col_val_in.1, s32[1024]{0:T(1024)} %near_row_in.1, ...), custom_call_target="tpu_custom_call" | custom-call | tf_op jit(solution)/shard_map/pallas_call | solution.py:439
  56.8 0.7 %copy.10 = bf16[512,256]{1,0:T(8,128)(2,1)} copy(bf16[512,256]{1,0:T(8,128)(2,1)S(1)} %shard_map.82) | data formatting | bytes 524288
